TPU v7x, 32 devices: a whole 2x2x4 slice. The times are simulated.
32 devices in a mesh: stream: 2 (over x), dp: 8 (over z, y), mp: 2 (over core).
Axes of the slice: x: 2, y: 2, z: 4, core: 2. Of those that a mesh axis runs over, the one named last changes fastest.
Arguments:
- inputs: bfloat16 [2, 8, 512, 768], P('stream', 'dp'), may hold values from -6 to 6
- w_query: bfloat16 [2, 2, 768, 768], P('stream', None, None, 'mp'), may hold values from -0.21875 to 0.21875
- w_key: bfloat16 [2, 2, 768, 768], P('stream', None, None, 'mp'), may hold values from -0.21875 to 0.21875
- w_value: bfloat16 [2, 2, 768, 768], P('stream', None, None, 'mp'), may hold values from -0.21875 to 0.21875
- w_out: bfloat16 [2, 2, 768, 768], P('stream', None, 'mp'), may hold values from -2.5 to 2.5
- w_up: bfloat16 [2, 2, 768, 3072], P('stream', None, None, 'mp'), may hold values from -0.21875 to 0.21875
- w_down: bfloat16 [2, 2, 3072, 768], P('stream', None, 'mp'), may hold values from -0.109375 to 0.109375
- norm_gain: float32 [2, 2, 2, 768], P('stream'), may hold values from 0.5 to 1.5
- norm_shift: float32 [2, 2, 2, 768], P('stream'), may hold values from -1.2 to 1.2
- box_table: float32 [2, 2, 12, 64], P('stream', None, 'mp'), may hold values from -4 to 4
- boxes: int32 [2, 2, 8, 512], P('stream', None, 'dp'), may hold values from 0 to 32
- pages: int32 [2, 8, 512], P(None, 'dp'), may hold values from 0 to 3, as said below
- cotangent: bfloat16 [2, 8, 512, 768], P('stream', 'dp'), may hold values from -6 to 6
Outputs:
- output: bfloat16 [2, 8, 512, 768], P('stream', 'dp')
- grad_inputs: float32 [2, 8, 512, 768], P('stream', 'dp')
- grad_query: float32 [2, 2, 768, 768], P('stream', None, 'dp', 'mp')
- grad_key: float32 [2, 2, 768, 768], P('stream', None, 'dp', 'mp')
- grad_value: float32 [2, 2, 768, 768], P('stream', None, 'dp', 'mp')
- grad_out: float32 [2, 2, 768, 768], P('stream', None, 'mp', 'dp')
- grad_up: float32 [2, 2, 768, 3072], P('stream', None, 'dp', 'mp')
- grad_down: float32 [2, 2, 3072, 768], P('stream', None, 'mp', 'dp')
- grad_gain: float32 [2, 2, 2, 768], P('stream', None, None, 'dp')
- grad_shift: float32 [2, 2, 2, 768], P('stream', None, None, 'dp')
- grad_table: float32 [2, 2, 12, 64], P('stream', None, 'mp', 'dp')
Inputs may be any that keep to these rules, and one draw needn't show every extreme that they name: `pages`: along each row of each stream the page number never falls, and every page number from 0 to 3 occurs in that row of both streams.
All inputs are finite; a program needn't handle non-finite values.
Results may differ from a plain program's by a relative error of at most 0.038.
Values may be sent and summed in bfloat16 or wider, within the bound.
No kernel may reach another device: no remote copies, remote signals or barrier semaphores. Data moves between devices by JAX's collectives and lax.ppermute only.
A program may use at most 320 MiB of HBM per device.

v0:
```python
import jax
import jax.numpy as jnp
from jax import lax
from jax.sharding import PartitionSpec as P

HEAD_DIM = 64


EPSILON = 1e-05
MASKED = -1e30
HIGHEST = lax.Precision.HIGHEST
LOWTYPE = jnp.bfloat16


def swapped(block, axis, stride):
    count = lax.axis_size(axis)
    route = []
    for low in range(count):
        high = low | 1 << stride
        if high != low and high < count:
            route += [(low, high), (high, low)]
    return lax.ppermute(block, axis, route)


def layer_norm(values, gain, shift):
    center = values - jnp.mean(values, -1, keepdims=True)
    spread = jnp.mean(center * center, -1, keepdims=True)
    return center * lax.rsqrt(spread + EPSILON) * gain + shift


def gelu_exact(values):
    return jax.nn.gelu(values, approximate=False)


def group_part(values):
    return values.astype(LOWTYPE).astype(jnp.float32)


def apply_forward(left, weight):
    return jnp.einsum("rsa,ab->rsb", left, weight, preferred_element_type=jnp.float32)


def apply_back(grad, weight):
    return jnp.einsum("rsb,ab->rsa", grad, weight, preferred_element_type=jnp.float32)


def contract(left, right):
    return jnp.einsum("rsa,rsb->ab", left, right, preferred_element_type=jnp.float32)


def split_heads(values, head_dim):
    return values.reshape(values.shape[0], values.shape[1], -1, head_dim)


def join_heads(values):
    return values.reshape(values.shape[0], values.shape[1], -1)


def score_block(queries, keys, bias, allowed, scale):
    raw = jnp.einsum("rqhd,rkhd->rhqk", queries, keys, preferred_element_type=jnp.float32) * scale
    return jnp.where(allowed[:, None], raw + bias, MASKED)


def bucket_select(buckets):
    marks = jnp.arange(buckets + 1, dtype=jnp.int32)
    index = jnp.clip(marks[:, None] - marks[None, :], -buckets, buckets - 1) + buckets
    slots = jnp.arange(2 * buckets, dtype=jnp.int32)
    return (index[:, :, None] == slots[None, None, :]).astype(jnp.float32)


def bucket_index(coords, buckets):
    return jnp.clip(coords[:, :, None] - coords[:, None, :], -buckets, buckets - 1) + buckets


def split_einsum(form, values, onehot):
    upper = values.astype(LOWTYPE)
    lower = (values - upper.astype(jnp.float32)).astype(LOWTYPE)
    return jnp.einsum(form, upper, onehot, preferred_element_type=jnp.float32) + jnp.einsum(
        form, lower, onehot, preferred_element_type=jnp.float32
    )


def body(
    inputs,
    w_query,
    w_key,
    w_value,
    w_out,
    w_up,
    w_down,
    norm_gain,
    norm_shift,
    box_table,
    boxes,
    pages,
    cotangent,
):
    side = lax.axis_index("stream")
    own_pages = lax.dynamic_index_in_dim(pages, side, 0, keepdims=False)
    far_pages = lax.dynamic_index_in_dim(pages, 1 - side, 0, keepdims=False)
    head_dim = HEAD_DIM
    scale = head_dim ** (-0.5)
    buckets = box_table.shape[3] // 2
    levels = buckets + 1
    select = bucket_select(buckets)
    marks = jnp.arange(levels, dtype=jnp.int32)
    onehot = jnp.concatenate(
        [
            (boxes[0, 0][:, :, None] == marks).astype(LOWTYPE),
            (boxes[0, 1][:, :, None] == marks).astype(LOWTYPE),
        ],
        axis=2,
    )
    index_x = bucket_index(boxes[0, 0], buckets)
    index_y = bucket_index(boxes[0, 1], buckets)
    box_bias = jnp.transpose(
        jnp.take(box_table[0, 0], index_x, axis=1) + jnp.take(box_table[0, 1], index_y, axis=1),
        (1, 0, 2, 3),
    )
    hidden = inputs[0].astype(jnp.float32)
    saved = []
    for layer in range(2):
        rounded = hidden.astype(LOWTYPE)
        queries = apply_forward(rounded, w_query[0, layer]).astype(LOWTYPE)
        keys = apply_forward(rounded, w_key[0, layer]).astype(LOWTYPE)
        values = apply_forward(rounded, w_value[0, layer]).astype(LOWTYPE)
        if layer == 1:
            keys_far, values_far = swapped((keys, values), "stream", 0)
            allowed = own_pages[:, :, None] == far_pages[:, None, :]
            bias = 0.0
        else:
            keys_far, values_far = (keys, values)
            allowed = own_pages[:, :, None] == own_pages[:, None, :]
            bias = box_bias
        query_heads = split_heads(queries, head_dim)
        key_heads = split_heads(keys_far, head_dim)
        value_heads = split_heads(values_far, head_dim)
        scores = score_block(query_heads, key_heads, bias, allowed, scale)
        top = jnp.max(scores, -1, keepdims=True)
        weights = jnp.exp(scores - top)
        total = jnp.sum(weights, -1, keepdims=True)
        probs = (weights / total).astype(LOWTYPE)
        log_total = top + jnp.log(total)
        context = join_heads(
            jnp.einsum("rhqk,rkhd->rqhd", probs, value_heads, preferred_element_type=jnp.float32)
        ).astype(LOWTYPE)
        attention = lax.psum(
            group_part(apply_forward(context, w_out[0, layer])).astype(jnp.bfloat16), "mp"
        ).astype(jnp.float32)
        mixed = hidden + attention
        middle = layer_norm(mixed, norm_gain[0, layer, 0], norm_shift[0, layer, 0])
        middle_low = middle.astype(LOWTYPE)
        upward = apply_forward(middle_low, w_up[0, layer])
        active = gelu_exact(upward).astype(LOWTYPE)
        feed = lax.psum(
            group_part(apply_forward(active, w_down[0, layer])).astype(jnp.bfloat16), "mp"
        ).astype(jnp.float32)
        combined = middle + feed
        saved.append(
            (
                rounded,
                query_heads,
                key_heads,
                value_heads,
                bias,
                allowed,
                log_total,
                context,
                mixed,
                middle_low,
                upward,
                active,
                combined,
            )
        )
        hidden = layer_norm(combined, norm_gain[0, layer, 1], norm_shift[0, layer, 1])
    output = hidden.astype(LOWTYPE)[None]
    grad = cotangent[0].astype(jnp.float32)
    layer_grads = [None, None]
    grad_table = None
    for layer in (1, 0):
        (
            rounded,
            query_heads,
            key_heads,
            value_heads,
            bias,
            allowed,
            log_total,
            context,
            mixed,
            middle_low,
            upward,
            active,
            combined,
        ) = saved[layer]
        unused, norm_pull = jax.vjp(
            layer_norm, combined, norm_gain[0, layer, 1], norm_shift[0, layer, 1]
        )
        grad_combined, gain_late, shift_late = norm_pull(grad)
        down_cot = grad_combined.astype(LOWTYPE)
        grad_wd = contract(active, down_cot)
        grad_active = apply_back(down_cot, w_down[0, layer])
        unused, gelu_pull = jax.vjp(gelu_exact, upward)
        grad_upward = gelu_pull(grad_active)[0].astype(LOWTYPE)
        grad_wu = contract(middle_low, grad_upward)
        grad_middle = grad_combined + lax.psum(
            group_part(apply_back(grad_upward, w_up[0, layer])).astype(jnp.bfloat16), "mp"
        ).astype(jnp.float32)
        unused, norm_pull = jax.vjp(
            layer_norm, mixed, norm_gain[0, layer, 0], norm_shift[0, layer, 0]
        )
        grad_mixed, gain_early, shift_early = norm_pull(grad_middle)
        out_cot = grad_mixed.astype(LOWTYPE)
        grad_wo = contract(context, out_cot)
        grad_context = split_heads(apply_back(out_cot, w_out[0, layer]).astype(LOWTYPE), head_dim)
        scores = score_block(query_heads, key_heads, bias, allowed, scale)
        probs_full = jnp.exp(scores - log_total)
        probs = probs_full.astype(LOWTYPE)
        grad_values_far = join_heads(
            jnp.einsum("rhqk,rqhd->rkhd", probs, grad_context, preferred_element_type=jnp.float32)
        ).astype(LOWTYPE)
        grad_probs = jnp.einsum(
            "rqhd,rkhd->rhqk", grad_context, value_heads, preferred_element_type=jnp.float32
        )
        grad_scores = probs_full * (
            grad_probs - jnp.sum(grad_probs * probs_full, -1, keepdims=True)
        )
        score_cot = grad_scores.astype(LOWTYPE)
        grad_queries = join_heads(
            jnp.einsum("rhqk,rkhd->rqhd", score_cot, key_heads, preferred_element_type=jnp.float32)
            * scale
        ).astype(LOWTYPE)
        grad_keys_far = join_heads(
            jnp.einsum(
                "rhqk,rqhd->rkhd", score_cot, query_heads, preferred_element_type=jnp.float32
            )
            * scale
        ).astype(LOWTYPE)
        if layer == 1:
            grad_keys, grad_values = swapped((grad_keys_far, grad_values_far), "stream", 0)
        else:
            grad_keys, grad_values = (grad_keys_far, grad_values_far)
            spread_grad = split_einsum("rhqk,rkb->rhqb", grad_scores, onehot)
            grad_block = split_einsum("rhqb,rqa->hab", spread_grad, onehot)
            grad_tx = jnp.einsum(
                "abt,hab->ht", select, grad_block[:, :levels, :levels], precision=HIGHEST
            )
            grad_ty = jnp.einsum(
                "abt,hab->ht", select, grad_block[:, levels:, levels:], precision=HIGHEST
            )
            grad_table = jnp.stack([grad_tx, grad_ty])[None]
        grad_wq = contract(rounded, grad_queries)
        grad_wk = contract(rounded, grad_keys)
        grad_wv = contract(rounded, grad_values)
        partial_value = (
            apply_back(grad_queries, w_query[0, layer])
            + apply_back(grad_keys, w_key[0, layer])
            + apply_back(grad_values, w_value[0, layer])
        )
        grad = grad_mixed + lax.psum(group_part(partial_value).astype(jnp.bfloat16), "mp").astype(
            jnp.float32
        )
        gains = jnp.stack([gain_early, gain_late])
        shifts = jnp.stack([shift_early, shift_late])
        layer_grads[layer] = (grad_wq, grad_wk, grad_wv, grad_wo, grad_wu, grad_wd, gains, shifts)
    stacked = [
        jnp.stack([first, second])[None] for first, second in zip(layer_grads[0], layer_grads[1])
    ]
    results = (
        lax.psum_scatter(stacked[0], "dp", scatter_dimension=2, tiled=True),
        lax.psum_scatter(stacked[1], "dp", scatter_dimension=2, tiled=True),
        lax.psum_scatter(stacked[2], "dp", scatter_dimension=2, tiled=True),
        lax.psum_scatter(stacked[3], "dp", scatter_dimension=3, tiled=True),
        lax.psum_scatter(stacked[4], "dp", scatter_dimension=2, tiled=True),
        lax.psum_scatter(stacked[5], "dp", scatter_dimension=3, tiled=True),
        lax.psum_scatter(stacked[6], "dp", scatter_dimension=3, tiled=True),
        lax.psum_scatter(stacked[7], "dp", scatter_dimension=3, tiled=True),
        lax.psum_scatter(grad_table, "dp", scatter_dimension=3, tiled=True),
    )
    return (
        output,
        grad[None],
        results[0],
        results[1],
        results[2],
        results[3],
        results[4],
        results[5],
        results[6],
        results[7],
        results[8],
    )


def solution(mesh):
    in_specs = (
        P("stream", "dp", None, None),
        P("stream", None, None, "mp"),
        P("stream", None, None, "mp"),
        P("stream", None, None, "mp"),
        P("stream", None, "mp", None),
        P("stream", None, None, "mp"),
        P("stream", None, "mp", None),
        P("stream", None, None, None),
        P("stream", None, None, None),
        P("stream", None, "mp", None),
        P("stream", None, "dp", None),
        P(None, "dp", None),
        P("stream", "dp", None, None),
    )
    out_specs = (
        P("stream", "dp", None, None),
        P("stream", "dp", None, None),
        P("stream", None, "dp", "mp"),
        P("stream", None, "dp", "mp"),
        P("stream", None, "dp", "mp"),
        P("stream", None, "mp", "dp"),
        P("stream", None, "dp", "mp"),
        P("stream", None, "mp", "dp"),
        P("stream", None, None, "dp"),
        P("stream", None, None, "dp"),
        P("stream", None, "mp", "dp"),
    )
    return jax.shard_map(body, mesh=mesh, in_specs=in_specs, out_specs=out_specs, check_vma=False)
```

profile of v0, /device:TPU:0, one launch (start us, length us, event | category | flops | bytes accessed | tf_op | source)
XLA Modules:
  0.0 3113.4 jit_solution(2731812452765635601)
XLA Ops:
  11.8 865.7 %gather_fusion = f32[262144,6]{1,0:T(8,128)} fusion(f32[6,64]{0,1:T(8,128)S(1)} %bitcast.417, s32[262144]{0:T(1024)S(1)} %broadcast_clamp_fusion.1), kind=kCustom, calls=%fused_computation.clone | custom fusion | bytes 13631488 | tf_op jit(solution)/shard_map/jit(_take)/gather | solution.py:117
  877.5 72.0 %copy.85 = f32[512,512,6]{0,1,2:T(8,128)} copy(f32[512,512,6]{2,1,0:T(8,128)} %bitcast.12) | data formatting | bytes 12582912 | tf_op jit(solution)/shard_map/jit(_take)/gather | solution.py:117
  950.1 865.7 %gather_fusion.1 = f32[262144,6]{1,0:T(8,128)} fusion(f32[6,64]{0,1:T(8,128)S(1)} %bitcast.418, s32[262144]{0:T(1024)S(1)} %broadcast_clamp_fusion), kind=kCustom, calls=%fused_computation.1.clone | custom fusion | bytes 13631488 | tf_op jit(solution)/shard_map/jit(_take)/gather | solution.py:117
  1815.7 72.2 %copy.89 = f32[512,512,6]{0,1,2:T(8,128)} copy(f32[512,512,6]{2,1,0:T(8,128)} %bitcast.18) | data formatting | bytes 12582912 | tf_op jit(solution)/shard_map/jit(_take)/gather | solution.py:117
  1894.4 6.1 fusion.216
  1907.6 21.2 all-reduce.17.cloned.1.call-done
  1932.4 11.5 multiply_convert_fusion.2
  1947.4 20.5 all-reduce.19.cloned.1.call-done
  1976.3 7.4 collective-permute-done.1
  1993.4 4.1 fusion.107
  2000.2 20.1 all-reduce.21.cloned.1.call-done
  2022.5 11.2 multiply_convert_fusion.1
  2039.1 18.6 all-reduce.23.cloned.1.call-done
  2063.3 4.4 add_convert_fusion.1
  2074.8 5.5 convolution_bitcast_fusion
  2080.3 11.5 all-reduce.25.cloned.1.call-done
  2091.8 3.1 multiply_reduce_fusion.2
  2095.6 3.1 fusion.206
  2111.5 15.9 collective-permute-done.2
  2131.9 2.7 convolution_bitcast_fusion.6
  2139.3 11.6 all-reduce.27.cloned.1.call-done
  2151.0 2.6 multiply_reduce_fusion.3
  2155.2 4.6 add_convert_fusion
  2161.1 2.3 fusion.89
  2165.0 2.9 convolution_bitcast_fusion.1
  2167.9 6.5 maximum_bitcast_fusion.1
  2174.5 15.1 copy.107
  2189.7 2.7 multiply_reduce_fusion.4
  2196.5 4.3 multiply_reduce_fusion
  2211.1 2.3 reshape.1388
  2214.5 2.8 convolution_bitcast_fusion.9
  2223.3 2.3 reshape.1386
  2225.7 3.6 fusion.93
  2229.3 3.2 maximum_bitcast_fusion.5
  2232.6 3.2 maximum_bitcast_fusion.4
  2235.8 5.3 copy.106
  2241.1 5.4 copy.105
  2249.8 5.4 copy.103
  2258.4 5.3 copy.101
  2264.5 3.7 convolution_bitcast_fusion.2
  2269.9 4.4 maximum_bitcast_fusion
  2276.9 6.6 fusion.14
  2286.1 21.9 all-reduce.5
  2310.3 30.1 reduce-scatter.11.cloned.1.call-done
  2341.9 19.0 all-reduce.31.cloned.1.call-done
  2360.9 2.5 add_bitcast_fusion
  2363.4 576.5 %all-reduce.33.cloned.1.call-done = (f32[1,2,768,384]{3,1,0,2:T(2,128)}, f32[1,2,768,384]{3,1,0,2:T(2,128)}, f32[1,2,768,384]{3,1,0,2:T(2,128)}, f32[1,2,384,768]{2,1,0,3:T(2,128)}, f32[1,2,1536,768]{2,1,0,3:T(2,128)}) async-done(((f32[1,2,768,384]{3,1,0,2:T(2,128)}, f32[1,2,768,384]{3,1,0,2:T(2,128)}, f32[1,2,768,384]{3,1,0,2:T(2,128)}, f32[1,2,384,768]{2,1,0,3:T(2,128)}, f32[1,2,1536,768]{2,1,0,3:T(2,128)}), ...) | async-done | bytes 18874384
  2949.5 156.8 %reduce-scatter.9.cloned.1.call-done = f32[1,2,96,1536]{3,2,1,0:T(8,128)} async-done(((f32[1,2,768,1536]{3,2,1,0:T(8,128)}), f32[1,2,96,1536]{3,2,1,0:T(8,128)}) %reduce-scatter.9.cloned.1.call-update) | async-done | bytes 1179664 | tf_op jit(solution)/shard_map/reduce_scatter | solution.py:275
  (457 shorter events, 140.7 us)
Async XLA Ops:
  7.2 1921.6 %all-reduce.17.cloned.1.call-start = ((), (), s32[]{:S(2)}) async-start(), calls=%async_computation.3 | async-start | bytes 1572864 | tf_op jit(solution)/shard_map/psum | solution.py:147
  1815.7 72.2 %copy-start.55 = (pred[512,512]{1,0:T(8,128)(4,1)S(1)}, pred[512,512]{1,0:T(8,128)(4,1)}, u32[]{:S(2)}) copy-start(pred[512,512]{1,0:T(8,128)(4,1)} %fusion.121) | copy-start | bytes 786436
  1815.7 72.6 %copy-start.56 = (pred[512,512]{1,0:T(8,128)(4,1)S(1)}, pred[512,512]{1,0:T(8,128)(4,1)}, u32[]{:S(2)}) copy-start(pred[512,512]{1,0:T(8,128)(4,1)} %fusion.120) | copy-start | bytes 786436
  1815.7 73.0 %copy-start.3 = (bf16[1,1,512,768]{3,2,1,0:T(8,128)(2,1)S(1)}, bf16[1,1,512,768]{3,2,1,0:T(8,128)(2,1)}, u32[]{:S(2)}) copy-start(bf16[1,1,512,768]{3,2,1,0:T(8,128)(2,1)} %param.15) | copy-start | bytes 2359300
  1905.2 39.8 %slice-start.4 = ((s8[4718592]{0:T(1024)(128)(4,1)}), s8[524288]{0:T(1024)(128)(4,1)S(1)}, s32[]{:S(2)}) async-start(s8[4718592]{0:T(1024)(128)(4,1)} %bitcast.467), calls=%async_computation.19 | async-start | bytes 1048576
  1906.7 61.2 %all-reduce.19.cloned.1.call-start = ((), (), s32[]{:S(2)}) async-start(), calls=%async_computation.4 | async-start | bytes 1572864 | tf_op jit(solution)/shard_map/psum | solution.py:155
  1907.6 60.3 %copy-start.76 = (f32[768]{0:T(1024)}, f32[768]{0:T(1024)S(1)}, u32[]{:S(2)}) copy-start(f32[768]{0:T(1024)S(1)} %get-tuple-element.109) | copy-start | bytes 9220
  1907.6 60.3 %copy-start.110 = (f32[768]{0:T(1024)}, f32[768]{0:T(1024)S(1)}, u32[]{:S(2)}) copy-start(f32[768]{0:T(1024)S(1)} %get-tuple-element.62) | copy-start | bytes 9220
  1907.6 62.5 %copy-start.65 = (f32[768]{0:T(1024)}, f32[768]{0:T(1024)S(1)}, u32[]{:S(2)}) copy-start(f32[768]{0:T(1024)S(1)} %get-tuple-element.110) | copy-start | bytes 9220
  1907.6 62.5 %copy-start.90 = (f32[768]{0:T(1024)}, f32[768]{0:T(1024)S(1)}, u32[]{:S(2)}) copy-start(f32[768]{0:T(1024)S(1)} %get-tuple-element.61) | copy-start | bytes 9220
  1930.2 37.6 %copy-start.81 = (f32[512]{0:T(512)}, f32[512]{0:T(512)S(1)}, u32[]{:S(2)}) copy-start(f32[512]{0:T(512)S(1)} %broadcast_multiply_fusion.3) | copy-start | bytes 6148
  1932.4 35.5 %copy-start.91 = (f32[512]{0:T(512)}, f32[512]{0:T(512)S(1)}, u32[]{:S(2)}) copy-start(f32[512]{0:T(512)S(1)} %fusion.183) | copy-start | bytes 6148
  1947.3 73.0 %all-reduce.21.cloned.1.call-start = ((), (), s32[]{:S(2)}) async-start(), calls=%async_computation.5 | async-start | bytes 1572864 | tf_op jit(solution)/shard_map/psum | solution.py:147
  1971.5 12.1 collective-permute-start.1
  1974.7 16.8 collective-permute-start
  1997.5 22.8 copy-start.66
  1997.5 22.8 copy-start.69
  1997.5 22.8 copy-start.87
  1999.7 22.8 copy-start.79
  1999.7 58.0 %all-reduce.23.cloned.1.call-start = ((), (), s32[]{:S(2)}) async-start(), calls=%async_computation.6 | async-start | bytes 1572864 | tf_op jit(solution)/shard_map/psum | solution.py:155
  2020.3 14.6 slice-start.6
  2022.1 35.6 %copy-start.84 = (f32[512]{0:T(512)}, f32[512]{0:T(512)S(1)}, u32[]{:S(2)}) copy-start(f32[512]{0:T(512)S(1)} %broadcast_multiply_fusion.1) | copy-start | bytes 6148
  2022.5 35.2 %copy-start.94 = (f32[512]{0:T(512)}, f32[512]{0:T(512)S(1)}, u32[]{:S(2)}) copy-start(f32[512]{0:T(512)S(1)} %fusion.185) | copy-start | bytes 6148
  2037.1 54.7 %all-reduce.25.cloned.1.call-start = ((), (), s32[]{:S(2)}) async-start(), calls=%async_computation.7 | async-start | bytes 1572864 | tf_op jit(solution)/shard_map/psum | solution.py:207
  2039.1 21.3 copy-start.89
  2071.2 79.7 %all-reduce.27.cloned.1.call-start = ((), (), s32[]{:S(2)}) async-start(), calls=%async_computation.8 | async-start | bytes 1572864 | tf_op jit(solution)/shard_map/psum | solution.py:261
  2106.7 20.7 copy-start.50
  2107.3 20.7 copy-start.25
  2107.6 20.5 collective-permute-start.3
  2109.4 18.0 collective-permute-start.2
  2110.2 18.6 copy-start.44
  2130.4 59.3 %all-reduce.29.cloned.1.call-start = ((), (), s32[]{:S(2)}) async-start(), calls=%async_computation.9 | async-start | bytes 1572864 | tf_op jit(solution)/shard_map/psum | solution.py:207
  2136.3 14.6 copy-start.67
  2136.3 14.6 copy-start.70
  2136.3 14.6 copy-start.88
  2136.3 14.6 copy-start.98
  2139.3 14.3 copy-start.107
  2163.4 145.3 %reduce-scatter.13.cloned.1.call-start = ((), (), s32[]{:S(2)}) async-start(), calls=%async_computation.13 | async-start | bytes 442368
  2174.5 15.2 copy-start.14
  2174.5 15.2 copy-start.77
  2174.5 15.2 copy-start.82
  2174.5 15.2 copy-start.92
  2213.4 126.9 %reduce-scatter.11.cloned.1.call-start = ((), (), s32[]{:S(2)}) async-start(), calls=%async_computation.12 | async-start | bytes 442368
  2225.7 135.2 %all-reduce.31.cloned.1.call-start = ((), (), s32[]{:S(2)}) async-start(), calls=%async_computation.10 | async-start | bytes 1572864 | tf_op jit(solution)/shard_map/psum | solution.py:261
  2232.5 707.4 %all-reduce.33.cloned.1.call-start = ((), (), s32[]{:S(2)}) async-start(), calls=%async_computation.14 | async-start | bytes 37748736
  2263.8 842.5 %reduce-scatter.9.cloned.1.call-start = ((), (), s32[]{:S(2)}) async-start(), calls=%async_computation.11 | async-start | bytes 10616832 | tf_op jit(solution)/shard_map/reduce_scatter | solution.py:275
  2284.2 76.7 %copy-start.12 = (f32[1,512,768]{2,1,0:T(8,128)S(1)}, f32[1,512,768]{2,1,0:T(8,128)}, u32[]{:S(2)}) copy-start(f32[1,512,768]{2,1,0:T(8,128)} %copy-done.11) | copy-start | bytes 4718596
  2284.2 76.7 %copy-start.102 = (f32[512]{0:T(512)S(1)}, f32[512]{0:T(512)}, u32[]{:S(2)}) copy-start(f32[512]{0:T(512)} %copy-done.101) | copy-start | bytes 6148
  (111 other events, 393.7 us)
Sparse Core Ops, SparseCore 0:
  1906.8 21.8 all-reduce.16
  1947.4 20.3 all-reduce.18
  1999.9 20.3 all-reduce.20
  2037.3 20.3 all-reduce.22
  2071.4 20.4 all-reduce.24
  2130.5 20.4 all-reduce.26
  2163.5 20.3 all-reduce.28
  2213.6 62.6 reduce-scatter.12
  2279.8 60.4 reduce-scatter.10
  2342.7 18.1 all-reduce.30
  2366.1 573.7 all-reduce.32
  2943.9 162.3 reduce-scatter.8
where the time goes:
time: 3130 us; the launch traced here: 3110 us
  local copies, waits for them, and re-layouts  1960 us (63%)
  waiting for transfers between devices  911 us (29%)
  matrix products  129 us (4%)
  other arithmetic  68.1 us (2%)
    gather x2, local copies, waits for them, and re-layouts, body(): jnp.take(box_table[0, 1], index_y, axis=1)  938 us
    gather x2, local copies, waits for them, and re-layouts, body(): jnp.take(box_table[0, 0], index_x, axis=1)  938 us
    unnamed x15, waiting for transfers between devices  607 us
    reduce_scatter x1, waiting for transfers between devices, body(): lax.psum_scatter(stacked[4], 'dp', scatter_dimension=2, tiled=True)  157 us
  transfers between devices with their start and end apart: 16, of which 13 were waited for; matrix products, arithmetic and copies ran while one was open for 5% of the time, Pallas kernels for 0%

commit v1 on v0

v1 whole, which is shorter than its diff:
```python
import functools

import jax
import jax.numpy as jnp
from jax import lax
from jax.experimental import pallas as pl
from jax.experimental.pallas import tpu as pltpu
from jax.sharding import PartitionSpec as P

HEAD_DIM = 64
EPSILON = 1e-05
MASKED = -1e30
LOW = jnp.bfloat16
F32 = jnp.float32
LANES = 128
HIGHEST = lax.Precision.HIGHEST
SCALE = HEAD_DIM ** (-0.5)


def dot(left, right):
    return lax.dot_general(left, right, (((1,), (0,)), ((), ())), preferred_element_type=F32)


def dot_nt(left, right):
    return lax.dot_general(left, right, (((1,), (1,)), ((), ())), preferred_element_type=F32)


def iota(shape, dim):
    return lax.broadcasted_iota(jnp.int32, shape, dim)


def normalized(values):
    center = values - jnp.mean(values, -1, keepdims=True)
    rstd = lax.rsqrt(jnp.mean(center * center, -1, keepdims=True) + EPSILON)
    return center * rstd, rstd


def norm_back(grad, xhat, rstd, gain):
    scaled = grad * gain
    grad_in = rstd * (
        scaled
        - jnp.mean(scaled, -1, keepdims=True)
        - xhat * jnp.mean(scaled * xhat, -1, keepdims=True)
    )
    return grad_in, jnp.sum(grad * xhat, 0, keepdims=True), jnp.sum(grad, 0, keepdims=True)


def call(kernel, outs, *args, smem=(), scratch=(), cost=None):
    in_specs = [
        pl.BlockSpec(memory_space=pltpu.SMEM if i in smem else pltpu.VMEM)
        for i in range(len(args))
    ]
    return pl.pallas_call(
        kernel,
        out_shape=[jax.ShapeDtypeStruct(s, d) for s, d in outs],
        in_specs=in_specs,
        out_specs=[pl.BlockSpec(memory_space=pltpu.VMEM)] * len(outs),
        scratch_shapes=list(scratch),
        compiler_params=pltpu.CompilerParams(vmem_limit_bytes=48 * 1024 * 1024),
        cost_estimate=cost,
    )(*args)


def cost_of(flops, nbytes):
    return pl.CostEstimate(flops=int(flops), bytes_accessed=int(nbytes), transcendentals=0)


def page_mask(cols, rows):
    return jnp.where(cols == rows, 0.0, MASKED).astype(F32)


def key_marks(cols, levels):
    lane = iota((cols.shape[0], LANES), 1)
    want = levels - lane % levels
    picked = jnp.where((lane // levels) % 2 == 0, cols[:, 0:1], cols[:, 1:2])
    return (picked == want).astype(F32).astype(LOW)


def query_marks(cols, levels):
    lane = iota((cols.shape[0], LANES), 1)
    hit = (lane == levels - cols[:, 0:1]) | (lane == levels + 40 - cols[:, 1:2])
    return hit.astype(F32).astype(LOW)


def bias_rows(table, head, levels):
    lane = iota((40, LANES), 1)
    blocks = []
    for dim in range(2):
        line = table[dim][head : head + 1, :]
        line = jnp.concatenate(
            [line, jnp.broadcast_to(line[:, -1:], (1, LANES - line.shape[1]))], axis=1
        )
        base = jnp.broadcast_to(pltpu.roll(line, LANES - levels, 1), (40, LANES))
        spread = pltpu.roll(base, 0, 1, stride=1, stride_axis=0)
        spread = jnp.where(lane < levels, spread - spread[:, levels : levels + 1], 0.0)
        upper = spread.astype(LOW).astype(F32)
        lower = spread - upper
        blocks.append(
            pltpu.roll(upper, dim * levels, 1) + pltpu.roll(lower, (2 + dim) * levels, 1)
            if dim
            else upper + pltpu.roll(lower, 2 * levels, 1)
        )
    blocks.append(jnp.zeros((LANES - 80, LANES), F32))
    return jnp.concatenate(blocks, axis=0).astype(LOW)


def half_masks():
    lane = iota((1, LANES), 1)
    first = (lane < HEAD_DIM).astype(F32).astype(LOW)
    return first, (1 - first.astype(F32)).astype(LOW)


def attend(q_ref, k_ref, v_ref, ext_ref, key_ext, mask, lse_ref, ctx_ref):
    seq, width = q_ref.shape
    halves = half_masks()
    lane = iota((seq, LANES), 1)
    ones = jnp.ones((seq, LANES), LOW)
    lse = jnp.zeros((seq, LANES), F32)
    for pair in range(width // LANES):
        at = slice(pair * LANES, (pair + 1) * LANES)
        queries, keys = q_ref[:, at], k_ref[:, at]
        if key_ext is not None:
            keys = jnp.concatenate([keys, key_ext], axis=1)
        values = jnp.concatenate([v_ref[:, at], ones], axis=1)
        parts = []
        for half in range(2):
            head = 2 * pair + half
            left = queries * halves[half]
            if key_ext is not None:
                left = jnp.concatenate([left, ext_ref[:, head * LANES : (head + 1) * LANES]], axis=1)
            scores = dot_nt(left, keys) + mask
            top = jnp.max(scores, -1, keepdims=True)
            weights = jnp.exp(scores - top).astype(LOW)
            out = dot(weights, values)
            total = out[:, LANES:]
            parts.append(out[:, :LANES] / total)
            lse = jnp.where(lane == head, top + jnp.log(total), lse)
        ctx_ref[:, at] = jnp.where(lane < HEAD_DIM, parts[0], parts[1]).astype(LOW)
    lse_ref[...] = lse


def first_attention(levels, x, wq, wk, wv, wo, cols, rows, table, part, q, k, v, lse, ctx, ext):
    states = x[...]
    q[...] = (dot(states, wq[...]).astype(LOW).astype(F32) * SCALE).astype(LOW)
    k[...] = dot(states, wk[...]).astype(LOW)
    v[...] = dot(states, wv[...]).astype(LOW)
    marks = query_marks(cols[...], levels)
    tables = [table[0], table[1]]
    for head in range(q.shape[1] // HEAD_DIM):
        ext[:, head * LANES : (head + 1) * LANES] = dot(
            marks, bias_rows(tables, head, levels)
        ).astype(LOW)
    mask = page_mask(cols[:, 2:3], rows[2:3, :])
    attend(q, k, v, ext, key_marks(cols[...], levels), mask, lse, ctx)
    part[...] = dot(ctx[...], wo[...]).astype(LOW)


def next_project(mixed, gain1, shift1, own, far, gain2, shift2, wq, wk, wv, combined, hidden, rounded, q, k, v):
    xhat, _ = normalized(mixed[...])
    total = xhat * gain1[...] + shift1[...] + (own[...].astype(F32) + far[...].astype(F32))
    combined[...] = total
    xhat, _ = normalized(total)
    state = xhat * gain2[...] + shift2[...]
    hidden[...] = state
    low = state.astype(LOW)
    rounded[...] = low
    k[...] = dot(low, wk[...]).astype(LOW)
    v[...] = dot(low, wv[...]).astype(LOW)
    q[...] = (dot(low, wq[...]).astype(LOW).astype(F32) * SCALE).astype(LOW)


def next_attention(q, k, v, wo, cols, rows, part, lse, ctx):
    mask = page_mask(cols[:, 2:3], rows[3:4, :])
    attend(q, k, v, None, None, mask, lse, ctx)
    part[...] = dot(ctx[...], wo[...]).astype(LOW)


def normal_cdf(values):
    return 0.5 * (1.0 + lax.erf(values * (0.5**0.5)))


def feed_forward(hidden, own, far, gain, shift, w_up, w_down, mixed, middle, upward, active, part):
    total = hidden[...].astype(F32) + (own[...].astype(F32) + far[...].astype(F32))
    mixed[...] = total
    xhat, _ = normalized(total)
    low = (xhat * gain[...] + shift[...]).astype(LOW)
    middle[...] = low
    step = 512
    acc = None
    for start in range(0, w_up.shape[1], step):
        at = slice(start, start + step)
        up = dot(low, w_up[:, at])
        upward[:, at] = up.astype(LOW)
        act = (up * normal_cdf(up)).astype(LOW)
        active[:, at] = act
        piece = dot(act, w_down[at, :])
        acc = piece if acc is None else acc + piece
    part[...] = acc.astype(LOW)


def feed_back_body(grad, combined, gain, w_up, w_down, upward, grad_comb, down_cot, grad_up, part, dgain, dshift):
    xhat, rstd = normalized(combined)
    grad_in, dgain[...], dshift[...] = norm_back(grad, xhat, rstd, gain)
    grad_comb[...] = grad_in
    low = grad_in.astype(LOW)
    down_cot[...] = low
    step = 512
    acc = None
    for start in range(0, w_up.shape[1], step):
        at = slice(start, start + step)
        back = dot_nt(low, w_down[at, :])
        up = upward[:, at].astype(F32)
        slope = normal_cdf(up) + up * (jnp.exp(-0.5 * up * up) * 0.3989422804014327)
        gup = (back * slope).astype(LOW)
        grad_up[:, at] = gup
        piece = dot_nt(gup, w_up[:, at])
        acc = piece if acc is None else acc + piece
    part[...] = acc.astype(LOW)


def last_feed_back(cot, mixed, gain1, shift1, own, far, gain, shift, w_up, w_down, upward, output, grad_comb, down_cot, grad_up, part, dgain, dshift):
    xhat, _ = normalized(mixed[...])
    combined = xhat * gain1[...] + shift1[...] + (own[...].astype(F32) + far[...].astype(F32))
    xhat, _ = normalized(combined)
    output[...] = (xhat * gain[...] + shift[...]).astype(LOW)
    feed_back_body(cot[...].astype(F32), combined, gain[...], w_up, w_down, upward, grad_comb, down_cot, grad_up, part, dgain, dshift)


def first_feed_back(grad_mixed, own, far, combined, gain, w_up, w_down, upward, grad_comb, down_cot, grad_up, part, dgain, dshift):
    grad = grad_mixed[...] + (own[...].astype(F32) + far[...].astype(F32))
    feed_back_body(grad, combined[...], gain[...], w_up, w_down, upward, grad_comb, down_cot, grad_up, part, dgain, dshift)


def attention_back_body(levels, page_row, grad_comb, own, far, mixed, gain, wo, q, k, v, lse, ctx, ext, cols, rows, grad_mixed, out_cot, gq, gkt, gvt, dgain, dshift, dtable):
    seq, width = q.shape
    grad = grad_comb[...] + (own[...].astype(F32) + far[...].astype(F32))
    xhat, rstd = normalized(mixed[...])
    grad_in, dgain[...], dshift[...] = norm_back(grad, xhat, rstd, gain[...])
    grad_mixed[...] = grad_in
    low = grad_in.astype(LOW)
    out_cot[...] = low
    gctx = dot_nt(low, wo[...]).astype(LOW)
    mask = page_mask(cols[:, 2:3], rows[page_row : page_row + 1, :])
    halves = half_masks()
    lane = iota((seq, LANES), 1)
    if ext is not None:
        key_ext = key_marks(cols[...], levels)
        back_ext = (
            (lane == levels - cols[:, 0:1]) | (lane == levels + HEAD_DIM - cols[:, 1:2])
        ).astype(F32).astype(LOW)
        line = iota((LANES, seq), 0)
        marks_t = ((line == rows[0:1, :]) | (line == rows[1:2, :] + HEAD_DIM)).astype(F32).astype(LOW)
        dtable[...] = jnp.zeros(dtable.shape, F32)
    for pair in range(width // LANES):
        at = slice(pair * LANES, (pair + 1) * LANES)
        queries, keys, values = q[:, at], k[:, at], v[:, at]
        gc = gctx[:, at]
        product = gc.astype(F32) * ctx[:, at].astype(F32)
        gc_t = jnp.transpose(gc)
        q_t = jnp.transpose(queries)
        keys_left = keys if ext is None else jnp.concatenate([keys, key_ext], axis=1)
        keys_right = keys if ext is None else jnp.concatenate([keys, back_ext], axis=1)
        parts = []
        for half in range(2):
            head = 2 * pair + half
            rows_at = slice(half * HEAD_DIM, (half + 1) * HEAD_DIM)
            out_at = slice(head * HEAD_DIM, (head + 1) * HEAD_DIM)
            left = queries * halves[half]
            if ext is not None:
                left = jnp.concatenate([left, ext[:, head * LANES : (head + 1) * LANES]], axis=1)
            scores = dot_nt(left, keys_left) + mask
            probs = jnp.exp(scores - lse[:, head : head + 1])
            delta = jnp.sum(
                jnp.where((lane < HEAD_DIM) == (half == 0), product, 0.0), -1, keepdims=True
            )
            grad_scores = probs * (dot_nt(gc * halves[half], values) - delta)
            score_cot = grad_scores.astype(LOW)
            gvt[out_at, :] = dot(gc_t[rows_at, :], probs.astype(LOW)).astype(LOW)
            gkt[out_at, :] = dot(q_t[rows_at, :], score_cot).astype(LOW)
            out = dot(score_cot, keys_right)
            parts.append(out[:, :LANES])
            if ext is not None:
                spread = out[:, LANES:]
                upper = spread.astype(LOW)
                lower = (spread - upper.astype(F32)).astype(LOW)
                block = dot(marks_t, upper) + dot(marks_t, lower)
                small = iota((40, LANES), 1)
                for dim in range(2):
                    piece = block[dim * HEAD_DIM : dim * HEAD_DIM + 40, :]
                    if dim:
                        piece = pltpu.roll(piece, HEAD_DIM, 1)
                    piece = jnp.where(small <= levels, piece, 0.0)
                    piece = pltpu.roll(piece, 0, 1, stride=1, stride_axis=0)
                    line = jnp.sum(piece, 0, keepdims=True)
                    over = pltpu.roll(line, LANES - 1, 1)
                    place = iota((1, LANES), 1)
                    line = jnp.where(place == 2 * levels - 1, line + over, line)
                    dtable[dim, head : head + 1, :] = line
        gq[:, at] = (jnp.where(lane < HEAD_DIM, parts[0], parts[1]) * SCALE).astype(LOW)


def next_attention_back(grad_comb, own, far, mixed, gain, wo, q, k, v, lse, ctx, cols, rows, grad_mixed, out_cot, gq, gkt, gvt, dgain, dshift):
    attention_back_body(0, 3, grad_comb, own, far, mixed, gain, wo, q, k, v, lse, ctx, None, cols, rows, grad_mixed, out_cot, gq, gkt, gvt, dgain, dshift, None)


def first_attention_back(levels, grad_comb, own, far, mixed, gain, wo, q, k, v, lse, ctx, ext, cols, rows, wq, wk, wv, grad_mixed, out_cot, gq, gkt, gvt, dgain, dshift, dtable, part):
    attention_back_body(levels, 2, grad_comb, own, far, mixed, gain, wo, q, k, v, lse, ctx, ext, cols, rows, grad_mixed, out_cot, gq, gkt, gvt, dgain, dshift, dtable)
    input_back(gq, gkt, gvt, wq, wk, wv, part)


def input_back(gq, gkt, gvt, wq, wk, wv, part):
    part[...] = (
        dot_nt(gq[...], wq[...])
        + dot_nt(jnp.transpose(gkt[...]), wk[...])
        + dot_nt(jnp.transpose(gvt[...]), wv[...])
    ).astype(LOW)


def feed_weights(down_cot, active, middle, grad_up, out):
    width = active.shape[1]
    step = 512
    left = jnp.transpose(down_cot[...])
    for start in range(0, width, step):
        out[:, start : start + step] = dot(left, active[:, start : start + step]).astype(LOW)
    left = jnp.transpose(middle[...])
    for start in range(0, width, step):
        out[:, width + start : width + start + step] = dot(
            left, grad_up[:, start : start + step]
        ).astype(LOW)


def attention_weights(rounded, gq, gkt, gvt, out_cot, ctx, out):
    width = gq.shape[1]
    left = jnp.transpose(rounded[...])
    out[:, :width] = dot(left, gq[...]).astype(LOW)
    out[:, width : 2 * width] = dot_nt(left, gkt[...]).astype(LOW)
    out[:, 2 * width : 3 * width] = dot_nt(left, gvt[...]).astype(LOW)
    left = jnp.transpose(out_cot[...])
    out[:, 3 * width :] = dot(left, ctx[...]).astype(LOW)


def other(block, axis):
    return lax.ppermute(block, axis, [(0, 1), (1, 0)])


def body(inputs, w_query, w_key, w_value, w_out, w_up, w_down, norm_gain, norm_shift, box_table, boxes, pages, cotangent):
    side = lax.axis_index("stream")
    _, rows_here, seq, d_model = inputs.shape
    assert rows_here == 1
    width = w_query.shape[3]
    hidden_width = w_up.shape[3]
    heads = width // HEAD_DIM
    levels = box_table.shape[3] // 2
    own_pages = lax.dynamic_index_in_dim(pages[:, 0], side, 0, keepdims=True)
    far_pages = lax.dynamic_index_in_dim(pages[:, 0], 1 - side, 0, keepdims=True)
    rows = jnp.concatenate([boxes[0, :, 0], own_pages, far_pages], axis=0)
    cols = jnp.transpose(rows)
    x = inputs[0, 0]
    gain = lambda layer, which: norm_gain[0, layer, which][None]
    shift = lambda layer, which: norm_shift[0, layer, which][None]
    wide = ((seq, d_model), F32)
    thin = ((seq, d_model), LOW)
    proj = ((seq, width), LOW)
    proj_t = ((width, seq), LOW)
    ff = ((seq, hidden_width), LOW)
    stats = ((seq, LANES), F32)
    vec = ((1, d_model), F32)

    part, q0, k0, v0, lse0, ctx0, ext0 = call(
        functools.partial(first_attention, levels),
        [thin, proj, proj, proj, stats, proj, ((seq, heads * LANES), LOW)],
        x, w_query[0, 0], w_key[0, 0], w_value[0, 0], w_out[0, 0], cols, rows, box_table[0],
    )
    mixed0, middle0, upward0, active0, feed = call(
        feed_forward, [wide, thin, ff, ff, thin],
        x, part, other(part, "mp"), gain(0, 0), shift(0, 0), w_up[0, 0], w_down[0, 0],
    )
    combined0, hidden1, rounded1, q1, k1, v1 = call(
        next_project, [wide, wide, thin, proj, proj, proj],
        mixed0, gain(0, 0), shift(0, 0), feed, other(feed, "mp"), gain(0, 1), shift(0, 1),
        w_query[0, 1], w_key[0, 1], w_value[0, 1],
    )
    k1, v1 = other(k1, "stream"), other(v1, "stream")
    part, lse1, ctx1 = call(next_attention, [thin, stats, proj], q1, k1, v1, w_out[0, 1], cols, rows)
    mixed1, middle1, upward1, active1, feed = call(
        feed_forward, [wide, thin, ff, ff, thin],
        hidden1, part, other(part, "mp"), gain(1, 0), shift(1, 0), w_up[0, 1], w_down[0, 1],
    )
    output, grad_comb, down_cot, grad_up, part, dgain11, dshift11 = call(
        last_feed_back, [thin, wide, thin, ff, thin, vec, vec],
        cotangent[0, 0], mixed1, gain(1, 0), shift(1, 0), feed, other(feed, "mp"), gain(1, 1), shift(1, 1),
        w_up[0, 1], w_down[0, 1], upward1,
    )
    (grads_ff1,) = call(
        feed_weights, [((d_model, 2 * hidden_width), LOW)], down_cot, active1, middle1, grad_up
    )
    grad_mixed, out_cot, gq, gkt, gvt, dgain10, dshift10 = call(
        next_attention_back, [wide, thin, proj, proj_t, proj_t, vec, vec],
        grad_comb, part, other(part, "mp"), mixed1, gain(1, 0), w_out[0, 1], q1, k1, v1, lse1, ctx1, cols, rows,
    )
    gkt, gvt = other(gkt, "stream"), other(gvt, "stream")
    (part,) = call(input_back, [thin], gq, gkt, gvt, w_query[0, 1], w_key[0, 1], w_value[0, 1])
    (grads_at1,) = call(
        attention_weights, [((d_model, 4 * width), LOW)], rounded1, gq, gkt, gvt, out_cot, ctx1
    )
    grad_comb, down_cot, grad_up, part, dgain01, dshift01 = call(
        first_feed_back, [wide, thin, ff, thin, vec, vec],
        grad_mixed, part, other(part, "mp"), combined0, gain(0, 1), w_up[0, 0], w_down[0, 0], upward0,
    )
    (grads_ff0,) = call(
        feed_weights, [((d_model, 2 * hidden_width), LOW)], down_cot, active0, middle0, grad_up
    )
    grad_mixed, out_cot, gq, gkt, gvt, dgain00, dshift00, dtable, part = call(
        functools.partial(first_attention_back, levels),
        [wide, thin, proj, proj_t, proj_t, vec, vec, ((2, 8, LANES), F32), thin],
        grad_comb, part, other(part, "mp"), mixed0, gain(0, 0), w_out[0, 0], q0, k0, v0, lse0, ctx0, ext0, cols, rows,
        w_query[0, 0], w_key[0, 0], w_value[0, 0],
    )
    (grads_at0,) = call(
        attention_weights, [((d_model, 4 * width), LOW)], x, gq, gkt, gvt, out_cot, ctx0
    )
    grad_inputs = grad_mixed + (part.astype(F32) + other(part, "mp").astype(F32))

    scatter = lambda block: lax.psum_scatter(block, "dp", scatter_dimension=0, tiled=True)
    ff1, at1, ff0, at0 = (scatter(g).astype(F32) for g in (grads_ff1, grads_at1, grads_ff0, grads_at0))
    n_dp = lax.axis_size("dp")
    vectors = jnp.concatenate(
        [dgain00, dgain01, dgain10, dgain11, dshift00, dshift01, dshift10, dshift11], axis=0
    )
    vectors = jnp.transpose(vectors.reshape(8, n_dp, d_model // n_dp), (1, 0, 2)).reshape(n_dp, -1)
    tables = dtable[:, :heads, : 2 * levels].reshape(2 * heads, n_dp, -1)
    tables = jnp.transpose(tables, (1, 0, 2)).reshape(n_dp, -1)
    small = scatter(jnp.concatenate([vectors, tables], axis=1).reshape(-1))
    cut = 8 * d_model // n_dp
    vectors = small[:cut].reshape(2, 2, 2, d_model // n_dp)
    grad_table = small[cut:].reshape(1, 2, heads, 2 * levels // n_dp)

    def columns(start, stop, a, b, flip=False):
        pair = (a[:, start:stop], b[:, start:stop])
        return jnp.stack([jnp.transpose(p) for p in pair] if flip else list(pair))[None]

    return (
        output[None, None],
        grad_inputs[None, None],
        columns(0, width, at0, at1),
        columns(width, 2 * width, at0, at1),
        columns(2 * width, 3 * width, at0, at1),
        columns(3 * width, 4 * width, at0, at1, True),
        columns(hidden_width, 2 * hidden_width, ff0, ff1),
        columns(0, hidden_width, ff0, ff1, True),
        vectors[:1],
        vectors[1:],
        grad_table,
    )


def solution(mesh):
    in_specs = (
        P("stream", "dp", None, None),
        P("stream", None, None, "mp"),
        P("stream", None, None, "mp"),
        P("stream", None, None, "mp"),
        P("stream", None, "mp", None),
        P("stream", None, None, "mp"),
        P("stream", None, "mp", None),
        P("stream", None, None, None),
        P("stream", None, None, None),
        P("stream", None, "mp", None),
        P("stream", None, "dp", None),
        P(None, "dp", None),
        P("stream", "dp", None, None),
    )
    out_specs = (
        P("stream", "dp", None, None),
        P("stream", "dp", None, None),
        P("stream", None, "dp", "mp"),
        P("stream", None, "dp", "mp"),
        P("stream", None, "dp", "mp"),
        P("stream", None, "mp", "dp"),
        P("stream", None, "dp", "mp"),
        P("stream", None, "mp", "dp"),
        P("stream", None, None, "dp"),
        P("stream", None, None, "dp"),
        P("stream", None, "mp", "dp"),
    )
    return jax.shard_map(body, mesh=mesh, in_specs=in_specs, out_specs=out_specs, check_vma=False)
```

time: 3130 us -> 497 us (0.16)
  local copies, waits for them, and re-layouts: 1960 us -> 41.3 us
  waiting for transfers between devices: 911 us -> 280 us
  matrix products: 129 us -> 0 us
  Pallas kernels: 0 us -> 95.3 us
  other arithmetic: 68.1 us -> 10.9 us
    gather x4 -> x0, local copies, waits for them, and re-layouts: 1880 us -> none  [the longest x2 938 us: body(): jnp.take(box_table[0, 1], index_y, axis=1)]
    unnamed x15 -> x4, waiting for transfers between devices: 607 us -> 0.07 us
    dot_general x54 -> x0, matrix products: 129 us -> none  [the longest x12 37.9 us: apply_forward(): jnp.einsum('rsa,ab->rsb', left, weight, preferred_element_type=jnp.float32)]
    psum x8 -> x0, waiting for transfers between devices: 122 us -> none  [the longest x2 41.2 us: body(): lax.psum(group_part(apply_forward(context, w_out[0, layer])).astype(jnp.b...]
    pallas_call x0 -> x14, Pallas kernels: none -> 95.3 us  [call(): pl.pallas_call(kernel, out_shape=[jax.ShapeDtypeStruct(s, d) for s, d in...]
    reduce_scatter x1 -> x4, waiting for transfers between devices: 157 us -> 232 us  [body(): lax.psum_scatter(block, 'dp', scatter_dimension=0, tiled=True)]
    broadcast_in_dim x5 -> x0, local copies, waits for them, and re-layouts: 36.5 us -> none  [body(): jnp.stack([first, second])[None]]
  transfers between devices with their start and end apart: 16 -> 16, of which waited for: 13 -> 13; matrix products, arithmetic and copies ran while one was open for 5% -> 4% of each run, Pallas kernels for 0% -> 7%
where the time goes in v1:
time: 497 us; the launch traced here: 487 us
  waiting for transfers between devices  280 us (56%)
  Pallas kernels  95.3 us (19%)
  local copies, waits for them, and re-layouts  41.3 us (8%)
  blocking collectives  37.8 us (8%)
  between operations  15.3 us (3%)
  other arithmetic  10.9 us (2%)
  starting transfers between devices  6.74 us (1%)
    reduce_scatter x4, waiting for transfers between devices, body(): lax.psum_scatter(block, 'dp', scatter_dimension=0, tiled=True)  232 us
    pallas_call x14, Pallas kernels, call(): pl.pallas_call(kernel, out_shape=[jax.ShapeDtypeStruct(s, d) for s, d in...  95.3 us
    ppermute x12, waiting for transfers between devices, other(): return lax.ppermute(block, axis, [(0, 1), (1, 0)])  48.2 us
    unnamed x1, blocking collectives  37.8 us
    unnamed x117, local copies, waits for them, and re-layouts  28.9 us
  transfers between devices with their start and end apart: 16, of which 13 were waited for; matrix products, arithmetic and copies ran while one was open for 4% of the time, Pallas kernels for 7%

profile of v1, /device:TPU:0, one launch (start us, length us, event | category | flops | bytes accessed | tf_op | source)
XLA Modules:
  0.0 487.2 jit_solution(10504980352016200187)
XLA Ops:
  8.9 1.5 slice_bitcast_fusion.8
  11.5 6.2 %shard_map.212 = (bf16[512,768]{1,0:T(8,128)(2,1)S(1)}, bf16[512,384]{1,0:T(8,128)(2,1)S(1)}, bf16[512,384]{1,0:T(8,128)(2,1)S(1)}, bf16[512,384]{1,0:T(8,128)(2...) custom-call(bf16[512,768]{1,0:T(8,128)(2,1)} %bitcast.107, ...), custom_call_target="tpu_custom_call" | custom-call | tf_op jit(solution)/shard_map/pallas_call | solution.py:53
  18.3 2.5 slice_bitcast_fusion
  20.9 5.0 %slice_bitcast_fusion.1 = (bf16[768,1536]{1,0:T(8,128)(2,1)}, bf16[768,1536]{1,0:T(8,128)(2,1)}) fusion(bf16[1,2,768,1536]{3,2,1,0:T(8,128)(2,1)} %param.18), kind=kLoop, calls=%fused_computation.1 | loop fusion | bytes 9437184 | tf_op jit(solution)/shard_map/squeeze | solution.py:387
  25.9 6.9 %shard_map.213 = (f32[512,768]{1,0:T(8,128)S(1)}, bf16[512,768]{1,0:T(8,128)(2,1)S(1)}, bf16[512,1536]{1,0:T(8,128)(2,1)}, bf16[512,1536]{1,0:T(8,128)(2,1)}, bf16[512,768]{1,0:T(8,128)(2,1)S(1)}) custom-call(bf16[512,768]{1,0:T(8,128)(2,1)S(1)} %bitcast.108, bf16[512,768]{1,0:T(8,128)(2,1)S(1)} %get-tuple-element.66.own, ...), custom_call_target="tpu_custom_call" | custom-call | tf_op jit(solution)/shard_map/pallas_call | solution.py:53
  32.8 1.1 copy-done.1
  35.3 1.9 collective-permute-done.1.far
  37.2 4.6 shard_map.214
  41.7 2.9 collective-permute-start.2
  44.6 9.9 %collective-permute-done.2.k = bf16[512,384]{1,0:T(8,128)(2,1)S(1)} collective-permute-done((bf16[512,384]{1,0:T(8,128)(2,1)S(1)}, bf16[512,384]{1,0:T(8,128)(2,1)S(1)}, u32[]{:S(2)}, u32[]{:S(2)}) %collective-permute-start.2) | collective-permute-done | bytes 393248 | tf_op jit(solution)/shard_map/ppermute | solution.py:343
  54.5 7.9 %collective-permute-done.3.v = bf16[512,384]{1,0:T(8,128)(2,1)S(1)} collective-permute-done((bf16[512,384]{1,0:T(8,128)(2,1)S(1)}, bf16[512,384]{1,0:T(8,128)(2,1)S(1)}, u32[]{:S(2)}, u32[]{:S(2)}) %collective-permute-start.3) | collective-permute-done | bytes 393248 | tf_op jit(solution)/shard_map/ppermute | solution.py:343
  62.4 3.1 shard_map.215
  65.6 2.3 collective-permute-done.4.far
  67.9 7.4 %shard_map.216 = (f32[512,768]{1,0:T(8,128)S(1)}, bf16[512,768]{1,0:T(8,128)(2,1)S(1)}, bf16[512,1536]{1,0:T(8,128)(2,1)}, bf16[512,1536]{1,0:T(8,128)(2,1)}, bf16[512,768]{1,0:T(8,128)(2,1)S(1)}) custom-call(f32[512,768]{1,0:T(8,128)} %get-tuple-element.69.hidden, bf16[512,768]{1,0:T(8,128)(2,1)S(1)} %get-tuple-element.73.own, ...), custom_call_target="tpu_custom_call" | custom-call | tf_op jit(solution)/shard_map/pallas_call | solution.py:53
  75.3 1.1 copy-done.2
  77.4 2.1 collective-permute-done.5.far
  79.6 8.9 %shard_map.217 = (bf16[512,768]{1,0:T(8,128)(2,1)}, f32[512,768]{1,0:T(8,128)S(1)}, bf16[512,768]{1,0:T(8,128)(2,1)S(1)}, bf16[512,1536]{1,0:T(8,128)(2,1)}, bf1...) custom-call(bf16[512,768]{1,0:T(8,128)(2,1)S(1)} %bitcast.110, f32[512,768]{1,0:T(8,128)} %copy-done.2, ...), custom_call_target="tpu_custom_call" | custom-call | tf_op jit(solution)/shard_map/pallas_call | solution.py:53
  88.5 1.2 copy-done.16
  90.7 2.2 collective-permute-done.6.far
  93.7 18.5 %shard_map.218 = (f32[512,768]{1,0:T(8,128)}, bf16[512,768]{1,0:T(8,128)(2,1)S(1)}, bf16[512,384]{1,0:T(8,128)(2,1)S(1)}, bf16[384,512]{1,0:T(8,128)(2,1)S(1)}, ...) custom-call(f32[512,768]{1,0:T(8,128)} %copy-done.16, ...), custom_call_target="tpu_custom_call" | custom-call | tf_op jit(solution)/shard_map/pallas_call | solution.py:53
  112.2 1.8 collective-permute-start.7
  114.3 9.9 %collective-permute-done.7.gkt = bf16[384,512]{1,0:T(8,128)(2,1)S(1)} collective-permute-done((bf16[384,512]{1,0:T(8,128)(2,1)S(1)}, bf16[384,512]{1,0:T(8,128)(2,1)S(1)}, u32[]{:S(2)}, u32[]{:S(2)}) %collective-permute-start.7) | collective-permute-done | bytes 393248 | tf_op jit(solution)/shard_map/ppermute | solution.py:343
  124.3 7.6 %collective-permute-done.8.gvt = bf16[384,512]{1,0:T(8,128)(2,1)S(1)} collective-permute-done((bf16[384,512]{1,0:T(8,128)(2,1)S(1)}, bf16[384,512]{1,0:T(8,128)(2,1)S(1)}, u32[]{:S(2)}, u32[]{:S(2)}) %collective-permute-start.8) | collective-permute-done | bytes 393248 | tf_op jit(solution)/shard_map/ppermute | solution.py:343
  131.9 3.3 shard_map.223
  141.5 1.4 shard_map.219.own
  143.0 2.3 collective-permute-done.9.far
  145.4 9.0 %shard_map.220 = (f32[512,768]{1,0:T(8,128)S(1)}, bf16[512,768]{1,0:T(8,128)(2,1)S(1)}, bf16[512,1536]{1,0:T(8,128)(2,1)}, bf16[512,768]{1,0:T(8,128)(2,1)S(1)},...) custom-call(f32[512,768]{1,0:T(8,128)} %get-tuple-element.82.grad_mixed, bf16[512,768]{1,0:T(8,128)(2,1)S(1)} %shard_map.219.own, ...), custom_call_target="tpu_custom_call" | custom-call | tf_op jit(solution)/shard_map/pallas_call | solution.py:53
  154.3 1.1 copy-done.13
  156.6 2.1 collective-permute-done.10.far
  159.6 13.2 %shard_map.221 = (f32[512,768]{1,0:T(8,128)}, bf16[512,768]{1,0:T(8,128)(2,1)}, bf16[512,384]{1,0:T(8,128)(2,1)S(1)}, bf16[384,512]{1,0:T(8,128)(2,1)S(1)}, bf16...) custom-call(f32[512,768]{1,0:T(8,128)} %copy-done.13, ...), custom_call_target="tpu_custom_call" | custom-call | tf_op jit(solution)/shard_map/pallas_call | solution.py:53
  172.7 1.2 copy-done.33
  173.9 3.2 shard_map.222
  177.2 1.3 copy-done.10
  178.5 1.1 copy-done.27
  179.7 1.1 copy-done.29
  180.8 4.8 shard_map.225
  185.7 1.3 copy-done.9
  187.5 1.1 copy-done.24
  188.7 1.1 copy-done.31
  189.8 4.9 shard_map.224
  194.7 1.1 copy-done.47
  197.6 37.8 %all-reduce = f32[6912]{0:T(1024)S(1)} all-reduce(f32[6912]{0:T(1024)S(1)} %reshape.61), channel_id=6, replica_groups=mesh['stream'=2,'dp'=8,'mp'=2] {'dp'}, use_global_device_ids=true, to_apply=%region_4.5.clone | all-reduce | flops 6912 | bytes 55296
  237.6 1.3 add_bitcast_fusion
  240.0 40.0 %reduce-scatter.5.cloned.1.call-done = bf16[96,1536]{1,0:T(8,128)(2,1)} async-done(((bf16[768,1536]{1,0:T(8,128)(2,1)}), bf16[96,1536]{1,0:T(8,128)(2,1)}) %reduce-scatter.5.cloned.1.call-update) | async-done | bytes 294928 | tf_op jit(solution)/shard_map/reduce_scatter | solution.py:424
  284.1 94.1 %reduce-scatter.11.cloned.1.call-done = bf16[96,3072]{1,0:T(8,128)(2,1)} async-done(((bf16[768,3072]{1,0:T(8,128)(2,1)}), bf16[96,3072]{1,0:T(8,128)(2,1)}) %reduce-scatter.11.cloned.1.call-update) | async-done | bytes 589840 | tf_op jit(solution)/shard_map/reduce_scatter | solution.py:424
  378.2 1.2 convert_element_type.23
  379.4 97.5 %reduce-scatter.9.cloned.1.call-done = bf16[96,3072]{1,0:T(8,128)(2,1)} async-done(((bf16[768,3072]{1,0:T(8,128)(2,1)}), bf16[96,3072]{1,0:T(8,128)(2,1)}) %reduce-scatter.9.cloned.1.call-update) | async-done | bytes 589840 | tf_op jit(solution)/shard_map/reduce_scatter | solution.py:424
  476.9 1.2 convert_element_type.22
  (159 shorter events, 27.6 us)
Async XLA Ops:
  7.2 3.2 copy-start.44
  7.2 231.7 %reduce-scatter.7.cloned.1.call-start = ((), (), s32[]{:S(2)}) async-start(), calls=%async_computation.5 | async-start | bytes 2654208 | tf_op jit(solution)/shard_map/reduce_scatter | solution.py:424
  8.9 1.7 copy-start.52
  8.9 1.7 copy-start.45
  8.9 2.0 copy-start.46
  10.4 7.9 %slice-start = ((s8[4718592]{0:T(1024)(128)(4,1)}), s8[4194304]{0:T(1024)(128)(4,1)S(1)}, s32[]{:S(2)}) async-start(s8[4718592]{0:T(1024)(128)(4,1)} %bitcast.113), calls=%async_computation.8 | async-start | bytes 8388608
  10.6 26.6 %copy-start.7 = (bf16[768,384]{1,0:T(8,128)(2,1)}, bf16[768,384]{1,0:T(8,128)(2,1)S(1)}, u32[]{:S(2)}) copy-start(bf16[768,384]{1,0:T(8,128)(2,1)S(1)} %get-tuple-element.168.wq) | copy-start | bytes 1769476
  10.9 7.4 %slice-start.1 = ((s8[4718592]{0:T(1024)(128)(4,1)}), s8[524288]{0:T(1024)(128)(4,1)S(1)}, s32[]{:S(2)}) async-start(s8[4718592]{0:T(1024)(128)(4,1)} %bitcast.113), calls=%async_computation.9 | async-start | bytes 1048576
  17.7 3.1 copy-start.14
  17.7 3.1 copy-start.25
  17.7 3.1 copy-start.35
  17.7 3.1 copy-start.37
  17.7 3.1 copy-start.39
  17.7 3.1 copy-start.41
  17.7 3.1 copy-start.50
  17.7 3.1 copy-start.51
  17.8 8.1 %collective-permute-start = (bf16[512,768]{1,0:T(8,128)(2,1)S(1)}, bf16[512,768]{1,0:T(8,128)(2,1)S(1)}, u32[]{:S(2)}, u32[]{:S(2)}) collective-permute-start(bf16[512,768]{1,0:T(8,128)(2,1)S(1)} %get-tuple-element.66.own), channel_id=1, source_target_pairs={{0,1},{1,0},{2,3},{3,2},{4,5},{5,4},{6,7},{7,6},{8,9},{9,8},{10,11... | collective-permute-start | bytes 2359304 | tf_op jit(solution)/shard_map/ppermute | solution.py:343
  20.8 5.1 %copy-start = (bf16[1,1,512,768]{3,2,1,0:T(8,128)(2,1)S(1)}, bf16[1,1,512,768]{3,2,1,0:T(8,128)(2,1)}, u32[]{:S(2)}) copy-start(bf16[1,1,512,768]{3,2,1,0:T(8,128)(2,1)} %param.13) | copy-start | bytes 2359300
  34.9 2.3 collective-permute-start.1
  41.7 12.8 %collective-permute-start.2 = (bf16[512,384]{1,0:T(8,128)(2,1)S(1)}, bf16[512,384]{1,0:T(8,128)(2,1)S(1)}, u32[]{:S(2)}, u32[]{:S(2)}) collective-permute-start(bf16[512,384]{1,0:T(8,128)(2,1)S(1)} %get-tuple-element.71), channel_id=1, source_target_pairs={{0,16},{16,0},{1,17},{17,1},{2,18},{18,2},{3,19},{19,3},{4,20},{20... | collective-permute-start | bytes 1179656 | tf_op jit(solution)/shard_map/ppermute | solution.py:343
  44.6 17.8 %collective-permute-start.3 = (bf16[512,384]{1,0:T(8,128)(2,1)S(1)}, bf16[512,384]{1,0:T(8,128)(2,1)S(1)}, u32[]{:S(2)}, u32[]{:S(2)}) collective-permute-start(bf16[512,384]{1,0:T(8,128)(2,1)S(1)} %get-tuple-element.72), channel_id=1, source_target_pairs={{0,16},{16,0},{1,17},{17,1},{2,18},{18,2},{3,19},{19,3},{4,20},{20... | collective-permute-start | bytes 1179656 | tf_op jit(solution)/shard_map/ppermute | solution.py:343
  65.6 2.4 collective-permute-start.4
  67.9 11.7 %copy-start.34 = (bf16[1,1,512,768]{3,2,1,0:T(8,128)(2,1)S(1)}, bf16[1,1,512,768]{3,2,1,0:T(8,128)(2,1)}, u32[]{:S(2)}) copy-start(bf16[1,1,512,768]{3,2,1,0:T(8,128)(2,1)} %param.25) | copy-start | bytes 2359300
  77.3 2.3 collective-permute-start.5
  90.5 2.3 collective-permute-start.6
  112.2 12.0 %collective-permute-start.7 = (bf16[384,512]{1,0:T(8,128)(2,1)S(1)}, bf16[384,512]{1,0:T(8,128)(2,1)S(1)}, u32[]{:S(2)}, u32[]{:S(2)}) collective-permute-start(bf16[384,512]{1,0:T(8,128)(2,1)S(1)} %get-tuple-element.84), channel_id=1, source_target_pairs={{0,16},{16,0},{1,17},{17,1},{2,18},{18,2},{3,19},{19,3},{4,20},{20... | collective-permute-start | bytes 1179656 | tf_op jit(solution)/shard_map/ppermute | solution.py:343
  114.0 17.8 %collective-permute-start.8 = (bf16[384,512]{1,0:T(8,128)(2,1)S(1)}, bf16[384,512]{1,0:T(8,128)(2,1)S(1)}, u32[]{:S(2)}, u32[]{:S(2)}) collective-permute-start(bf16[384,512]{1,0:T(8,128)(2,1)S(1)} %get-tuple-element.85), channel_id=1, source_target_pairs={{0,16},{16,0},{1,17},{17,1},{2,18},{18,2},{3,19},{19,3},{4,20},{20... | collective-permute-start | bytes 1179656 | tf_op jit(solution)/shard_map/ppermute | solution.py:343
  137.4 142.6 %reduce-scatter.5.cloned.1.call-start = ((), (), s32[]{:S(2)}) async-start(), calls=%async_computation.4 | async-start | bytes 2654208 | tf_op jit(solution)/shard_map/reduce_scatter | solution.py:424
  143.0 2.4 collective-permute-start.9
  145.3 14.2 %copy-start.4 = (bf16[384,768]{1,0:T(8,128)(2,1)S(1)}, bf16[384,768]{1,0:T(8,128)(2,1)}, u32[]{:S(2)}) copy-start(bf16[384,768]{1,0:T(8,128)(2,1)} %copy-done.3) | copy-start | bytes 1769476
  145.3 14.2 %copy-start.6 = (bf16[768,384]{1,0:T(8,128)(2,1)S(1)}, bf16[768,384]{1,0:T(8,128)(2,1)}, u32[]{:S(2)}) copy-start(bf16[768,384]{1,0:T(8,128)(2,1)} %copy-done.5) | copy-start | bytes 1769476
  145.3 14.2 %copy-start.15 = (bf16[512,384]{1,0:T(8,128)(2,1)S(1)}, bf16[512,384]{1,0:T(8,128)(2,1)}, u32[]{:S(2)}) copy-start(bf16[512,384]{1,0:T(8,128)(2,1)} %copy-done.14) | copy-start | bytes 1179652
  145.3 14.2 %copy-start.36 = (bf16[512,384]{1,0:T(8,128)(2,1)S(1)}, bf16[512,384]{1,0:T(8,128)(2,1)}, u32[]{:S(2)}) copy-start(bf16[512,384]{1,0:T(8,128)(2,1)} %copy-done.35) | copy-start | bytes 1179652
  145.3 14.2 %copy-start.38 = (bf16[512,384]{1,0:T(8,128)(2,1)S(1)}, bf16[512,384]{1,0:T(8,128)(2,1)}, u32[]{:S(2)}) copy-start(bf16[512,384]{1,0:T(8,128)(2,1)} %copy-done.37) | copy-start | bytes 1179652
  145.3 14.2 %copy-start.40 = (bf16[512,384]{1,0:T(8,128)(2,1)S(1)}, bf16[512,384]{1,0:T(8,128)(2,1)}, u32[]{:S(2)}) copy-start(bf16[512,384]{1,0:T(8,128)(2,1)} %copy-done.39) | copy-start | bytes 1179652
  145.4 14.2 %copy-start.42 = (f32[512,128]{1,0:T(8,128)S(1)}, f32[512,128]{1,0:T(8,128)}, u32[]{:S(2)}) copy-start(f32[512,128]{1,0:T(8,128)} %copy-done.41) | copy-start | bytes 786436
  156.4 2.3 copy-start.32
  156.4 2.3 collective-permute-start.10
  172.7 1.2 copy-start.33
  173.9 3.3 copy-start.11
  177.1 1.4 copy-start.10
  177.1 201.0 %reduce-scatter.11.cloned.1.call-start = ((), (), s32[]{:S(2)}) async-start(), calls=%async_computation.7 | async-start | bytes 5308416 | tf_op jit(solution)/shard_map/reduce_scatter | solution.py:424
  185.6 1.4 copy-start.9
  185.6 1.9 copy-start.12
  185.7 291.2 %reduce-scatter.9.cloned.1.call-start = ((), (), s32[]{:S(2)}) async-start(), calls=%async_computation.6 | async-start | bytes 5308416 | tf_op jit(solution)/shard_map/reduce_scatter | solution.py:424
  194.7 1.2 copy-start.53
  194.7 42.9 %copy-start.43 = (f32[512,768]{1,0:T(8,128)S(1)}, f32[512,768]{1,0:T(8,128)}, u32[]{:S(2)}) copy-start(f32[512,768]{1,0:T(8,128)} %get-tuple-element.96) | copy-start | bytes 4718596
  195.8 41.8 %collective-permute-start.11 = (bf16[512,768]{1,0:T(8,128)(2,1)S(1)}, bf16[512,768]{1,0:T(8,128)(2,1)S(1)}, u32[]{:S(2)}, u32[]{:S(2)}) collective-permute-start(bf16[512,768]{1,0:T(8,128)(2,1)S(1)} %copy-done.47), channel_id=1, source_target_pairs={{0,1},{1,0},{2,3},{3,2},{4,5},{5,4},{6,7},{7,6},{8,9},{9,8},{10,11... | collective-permute-start | bytes 2359304 | tf_op jit(solution)/shard_map/ppermute | solution.py:343
  (24 other events, 23.7 us)
Sparse Core Ops, SparseCore 0:
  137.6 70.7 reduce-scatter.6
  211.8 68.1 reduce-scatter.4
  283.7 94.4 reduce-scatter.10
  381.7 95.1 reduce-scatter.8
